TPU v7x, 32 devices: a whole 2x2x4 slice. The times are simulated.
32 devices in a mesh: parts: 2 (over x), row: 16 (over z, y, core).
Axes of the slice: x: 2, y: 2, z: 4, core: 2. Of those that a mesh axis runs over, the one named last changes fastest.
Arguments:
- z_left: bfloat16 [512, 256, 128], P(('parts', 'row')), parts along dimension 0, may hold values from -6 to 6
- z_right: bfloat16 [128, 256, 128], P(('parts', 'row')), parts along dimension 0, may hold values from -6 to 6
- pair_block: bfloat16 [512, 64, 128], P('parts', 'row'), parts along dimension 0, may hold values from -6 to 6
- row_valid: int32 [512], P(('parts', 'row')), parts along dimension 0, may hold values 0 or 1
- col_valid: int32 [128], P(('parts', 'row')), parts along dimension 0, may hold values 0 or 1
- k_valid: int32 [512], P('parts'), parts along dimension 0, may hold values 0 or 1
- in_gain: float32 [128], replicated, may hold values from 0.1 to 1.9
- w_left: bfloat16 [128, 256], replicated, may hold values from -0.5 to 0.5
- w_right: bfloat16 [128, 256], replicated, may hold values from -0.5 to 0.5
- w_gate: bfloat16 [128, 128], replicated, may hold values from -0.5 to 0.5
- w_out: bfloat16 [128, 128], replicated, may hold values from -0.5 to 0.5
- out_gain: float32 [128], replicated, may hold values from 0.1 to 1.9
Outputs:
- update: bfloat16 [512, 64, 128], P('parts', 'row'), parts along dimension 0
There are 2 independent parts, one for each index of `parts`. A program takes and returns all parts, laid end to end along the dimension named above; an argument that names none is the same for every part. Nothing has to cross between parts.
All inputs are finite; a program needn't handle non-finite values. No bound on the sum of `row_valid` or of `col_valid` on one device may be relied on, other than what follows from the above.
Results may differ from a plain program's by a relative error of at most 0.0081.
Values may be sent and summed in bfloat16 or wider, within the bound.
A program may use at most 320 MiB of HBM per device.

v0:
```python
import jax
import jax.numpy as jnp
from jax import lax
from jax.sharding import PartitionSpec as P


def layer_norm(values, scale_gain):
    average = jnp.mean(values, axis=-1, keepdims=True)
    centered = values - average
    variance = jnp.mean(centered * centered, axis=-1, keepdims=True)
    return centered / jnp.sqrt(variance + 1e-05) * scale_gain


def activations(raw_pairs, valid_rows, k_valid, in_gain, weight):
    row_count, width_k, channels = raw_pairs.shape
    normed = layer_norm(raw_pairs.astype(jnp.float32), in_gain).astype(jnp.bfloat16)
    projected = jnp.dot(
        normed.reshape(row_count * width_k, channels), weight, preferred_element_type=jnp.float32
    )
    projected = projected.reshape(row_count, width_k, -1)
    hidden = projected.shape[-1] // 2
    masking = valid_rows.astype(jnp.float32)[:, None] * k_valid.astype(jnp.float32)[None, :]
    return (
        jax.nn.sigmoid(projected[..., :hidden]) * projected[..., hidden:] * masking[..., None]
    ).astype(jnp.bfloat16)


def local(
    z_left,
    z_right,
    pair_block,
    row_valid,
    col_valid,
    k_valid,
    in_gain,
    w_left,
    w_right,
    w_gate,
    w_out,
    out_gain,
):
    left_act = activations(z_left, row_valid, k_valid, in_gain, w_left)
    right_act = activations(z_right, col_valid, k_valid, in_gain, w_right)
    hidden = left_act.shape[2]
    block_rows, block_cols, channels = pair_block.shape
    triangle = jnp.einsum(
        "ikc,jkc->ijc",
        left_act,
        lax.all_gather(right_act, "row", axis=0, tiled=True),
        preferred_element_type=jnp.float32,
    )
    tnorm = layer_norm(triangle, out_gain).astype(jnp.bfloat16)
    swapped = lax.all_to_all(tnorm, "row", split_axis=1, concat_axis=0, tiled=True)
    normed_block = layer_norm(pair_block.astype(jnp.float32), in_gain).astype(jnp.bfloat16)
    gate_value = jax.nn.sigmoid(
        jnp.dot(normed_block.reshape(-1, channels), w_gate, preferred_element_type=jnp.float32)
    )
    outward = jnp.dot(swapped.reshape(-1, hidden), w_out, preferred_element_type=jnp.float32)
    return (gate_value * outward).reshape(block_rows, block_cols, channels).astype(jnp.bfloat16)


def solution(mesh):
    placed = (
        P(("parts", "row"), None, None),
        P(("parts", "row"), None, None),
        P("parts", "row", None),
        P(("parts", "row")),
        P(("parts", "row")),
        P("parts"),
        P(),
        P(),
        P(),
        P(),
        P(),
        P(),
    )
    return jax.shard_map(
        local, mesh=mesh, in_specs=placed, out_specs=P("parts", "row", None), check_vma=False
    )
```

profile of v0, /device:TPU:1, one launch (start us, length us, event | category | flops | bytes accessed | tf_op | source)
XLA Modules:
  0.0 99.3 jit_solution(15399495277930093630)
XLA Ops:
  6.5 0.7 convert_element_type.48
  7.3 1.1 %convert_reduce_fusion.1 = f32[4,256]{1,0:T(4,128)S(1)} fusion(bf16[4,256,128]{2,1,0:T(8,128)(2,1)} %param.13), kind=kLoop, calls=%fused_computation.28 | loop fusion | flops 261120 | bytes 266240 | tf_op jit(solution)/shard_map/reduce_sum | solution.py:8
  8.4 0.0 copy-start.1
  8.4 1.4 %fusion.26 = f32[4,256]{1,0:T(4,128)S(1)} fusion(bf16[4,256,128]{2,1,0:T(8,128)(2,1)} %param.13, f32[4,256]{1,0:T(4,128)S(1)} %broadcast_multiply_fusion.5), kind=kLoop, calls=%fused_computation.38 | loop fusion | flops 523264 | bytes 270336 | tf_op jit(solution)/shard_map/reduce_sum | solution.py:10
  9.8 0.7 convert_element_type.47
  10.5 0.1 broadcast_multiply_fusion.4
  10.6 1.4 %fusion.34 = f32[4,256,256]{2,1,0:T(8,128)S(1)} fusion(bf16[4,256,128]{2,1,0:T(8,128)(2,1)} %param.13, f32[128]{0:T(128)} %param.18, f32[4,256]{1,0:T(4,128)S(1)} %add_sqrt_fusion.3, f32[4,256]{1,0:T(4,128)S(1)} %broadcast_multiply_fusion.5, bf16[128,256]{1,0:T(8,128)(2,1)} %param.20), kind=kOutput, calls=%fused_computation.48 | convolution fusion | flops 67764224 | bytes 1384960 | tf_op jit(solution)/shard_map/dot_general | solution.py:17
  12.0 0.0 copy-start.5
  12.0 0.9 fusion.30
  12.9 0.0 all-gather.2.cloned.1.call-update
  13.0 0.3 convert_reduce_fusion
  13.3 1.3 %fusion.2 = f32[16,256]{1,0:T(8,128)S(1)} fusion(bf16[16,256,128]{2,1,0:T(8,128)(2,1)S(1)} %copy-done.1, f32[16,256]{1,0:T(8,128)S(1)} %broadcast_multiply_fusion.2), kind=kLoop, calls=%fused_computation.4 | loop fusion | flops 2093056 | bytes 1081344 | tf_op jit(solution)/shard_map/reduce_sum | solution.py:10
  14.6 0.1 broadcast_multiply_fusion.1
  14.7 1.5 %fusion.14 = f32[16,256,256]{2,1,0:T(8,128)S(1)} fusion(bf16[16,256,128]{2,1,0:T(8,128)(2,1)S(1)} %copy-done.1, f32[128]{0:T(128)S(1)} %copy-done.5, f32[16,256]{1,0:T(8,128)S(1)} %add_sqrt_fusion.1, f32[16,256]{1,0:T(8,128)S(1)} %broadcast_multiply_fusion.2, bf16[128,256]{1,0:T(8,128)(2,1)S(1)} %copy-done), kind=kOutput, calls=%fused_computation.21 | convolution fusion | flops 271056896 | bytes 5341696 | tf_op jit(solution)/shard_map/dot_general | solution.py:17
  16.3 0.7 fusion.6
  17.0 0.0 copy-start.2
  17.0 0.9 copy.20
  17.9 0.0 copy-done.2
  17.9 0.3 convert_reduce_fusion.2
  18.3 0.6 fusion.25
  19.0 47.2 %all-gather.2.cloned.1.call-done = bf16[64,256,128]{2,1,0:T(8,128)(2,1)} async-done(((bf16[4,256,128]{2,1,0:T(8,128)(2,1)}), bf16[64,256,128]{2,1,0:T(8,128)(2,1)}) %all-gather.2.cloned.1.call-update) | async-done | bytes 4194320 | tf_op jit(solution)/shard_map/all_gather | solution.py:49
  66.2 6.8 %copy.19 = bf16[64,256,128]{1,0,2:T(8,128)(2,1)} copy(bf16[64,256,128]{2,1,0:T(8,128)(2,1)} %all-gather.2.cloned.1.call-done) | data formatting | bytes 8388608 | tf_op jit(solution)/shard_map/all_gather | solution.py:49
  73.0 3.4 %fusion.41 = (f32[16,64]{1,0:T(8,128)S(1)}, f32[16,64,128]{1,0,2:T(8,128)S(1)}) fusion(bf16[64,256,128]{1,0,2:T(8,128)(2,1)} %copy.19, bf16[16,256,128]{1,0,2:T(8,128)(2,1)S(1)} %copy.20), kind=kOutput, calls=%fused_computation.64 | convolution fusion | flops 67238912 | bytes 5771264 | tf_op jit(solution)/shard_map/ikc,jkc->ijc/dot_general | solution.py:46
  76.4 0.2 multiply_reduce_fusion
  76.6 0.2 multiply_convert_fusion
  76.8 1.3 %copy.21 = bf16[16,64,128]{2,0,1:T(8,128)(2,1)} copy(bf16[16,64,128]{1,0,2:T(8,128)(2,1)S(1)} %multiply_convert_fusion) | data formatting | bytes 524288 | tf_op jit(solution)/shard_map/convert_element_type | solution.py:52
  78.1 3.7 %all-to-all-start = ((bf16[16,64,128]{2,0,1:T(8,128)(2,1)}), bf16[16,64,128]{2,0,1:T(8,128)(2,1)S(1)}, u32[]{:S(2)}, u32[]{:S(2)}) async-start(bf16[16,64,128]{2,0,1:T(8,128)(2,1)} %copy.21), calls=%async_computation | async-start | bytes 524288 | tf_op jit(solution)/shard_map/all_to_all | solution.py:53
  81.8 0.7 fusion.24
  82.6 0.3 fusion.12
  82.8 8.5 %all-to-all-done = bf16[16,64,128]{2,0,1:T(8,128)(2,1)S(1)} async-done(((bf16[16,64,128]{2,0,1:T(8,128)(2,1)}), bf16[16,64,128]{2,0,1:T(8,128)(2,1)S(1)}, u32[]{:S(2)}, u32[]{:S(2)}) %all-to-all-start) | async-done | bytes 262176 | tf_op jit(solution)/shard_map/all_to_all | solution.py:53
  91.4 0.1 copy.22
  91.5 0.9 fusion.13
  (22 shorter events, 0.1 us)
Async XLA Ops:
  6.5 8.2 %copy-start = (bf16[128,256]{1,0:T(8,128)(2,1)S(1)}, bf16[128,256]{1,0:T(8,128)(2,1)}, u32[]{:S(2)}) copy-start(bf16[128,256]{1,0:T(8,128)(2,1)} %param.19) | copy-start | bytes 196612
  6.5 59.6 %all-gather.2.cloned.1.call-start = ((), (), s32[]{:S(2)}) async-start(), calls=%async_computation.1 | async-start | bytes 4456448 | tf_op jit(solution)/shard_map/all_gather | solution.py:49
  8.3 4.6 %copy-start.7 = (s32[16]{0:T(128)S(1)}, s32[16]{0:T(128)}, u32[]{:S(2)}) copy-start(s32[16]{0:T(128)} %param.15) | copy-start | bytes 196
  8.4 4.6 %copy-start.1 = (bf16[16,256,128]{2,1,0:T(8,128)(2,1)S(1)}, bf16[16,256,128]{2,1,0:T(8,128)(2,1)}, u32[]{:S(2)}) copy-start(bf16[16,256,128]{2,1,0:T(8,128)(2,1)} %param.12) | copy-start | bytes 3145732
  12.0 2.7 %copy-start.5 = (f32[128]{0:T(128)S(1)}, f32[128]{0:T(128)}, u32[]{:S(2)}) copy-start(f32[128]{0:T(128)} %param.18) | copy-start | bytes 1540
  17.0 1.0 copy-start.2
  73.0 3.6 %copy-start.4 = (f32[128]{0:T(128)S(1)}, f32[128]{0:T(128)}, u32[]{:S(2)}) copy-start(f32[128]{0:T(128)} %param.23) | copy-start | bytes 1540
  76.6 6.0 %copy-start.6 = (bf16[128,128]{1,0:T(8,128)(2,1)S(1)}, bf16[128,128]{1,0:T(8,128)(2,1)}, u32[]{:S(2)}) copy-start(bf16[128,128]{1,0:T(8,128)(2,1)} %param.21) | copy-start | bytes 98308
  78.1 13.4 %copy-start.3 = (bf16[128,128]{1,0:T(8,128)(2,1)S(1)}, bf16[128,128]{1,0:T(8,128)(2,1)}, u32[]{:S(2)}) copy-start(bf16[128,128]{1,0:T(8,128)(2,1)} %param.22) | copy-start | bytes 98308
  78.1 13.3 %all-to-all-start = ((bf16[16,64,128]{2,0,1:T(8,128)(2,1)}), bf16[16,64,128]{2,0,1:T(8,128)(2,1)S(1)}, u32[]{:S(2)}, u32[]{:S(2)}) async-start(bf16[16,64,128]{2,0,1:T(8,128)(2,1)} %copy.21), calls=%async_computation | async-start | bytes 524288 | tf_op jit(solution)/shard_map/all_to_all | solution.py:53
Sparse Core Ops, SparseCore 0:
  13.1 53.0 all-gather.1
where the time goes:
time: 100 us; the launch traced here: 99.3 us
  waiting for transfers between devices  55.7 us (56%)
  between operations  13.6 us (14%)
  other arithmetic  9.51 us (10%)
  local copies, waits for them, and re-layouts  9.19 us (9%)
  matrix products  7.54 us (8%)
  starting transfers between devices  3.71 us (4%)
    all_gather x1, waiting for transfers between devices, local(): lax.all_gather(right_act, 'row', axis=0, tiled=True)  47.2 us
    all_to_all x1, waiting for transfers between devices, local(): lax.all_to_all(tnorm, 'row', split_axis=1, concat_axis=0, tiled=True)  8.54 us
    all_gather x1, local copies, waits for them, and re-layouts, local(): lax.all_gather(right_act, 'row', axis=0, tiled=True)  6.82 us
    all_to_all x1, starting transfers between devices, local(): lax.all_to_all(tnorm, 'row', split_axis=1, concat_axis=0, tiled=True)  3.71 us
    reduce_sum x4, other arithmetic, layer_norm(): variance = jnp.mean(centered * centered, axis=-1, keepdims=True)  3.55 us
    dot_general x1, matrix products, local(): jnp.einsum('ikc,jkc->ijc', left_act, lax.all_gather(right_act, 'row', axi...  3.4 us
    dot_general x2, matrix products, activations(): jnp.dot(normed.reshape(row_count * width_k, channels), weight, preferred_...  2.93 us
  transfers between devices with their start and end apart: 2, of which 2 were waited for; matrix products, arithmetic and copies ran while one was open for 7% of the time, Pallas kernels for 0%

commit v1 on v0

v1 whole, which is shorter than its diff:
```python
import functools

import jax
import jax.numpy as jnp
from jax import lax
from jax.experimental import pallas as pl
from jax.experimental.pallas import tpu as pltpu
from jax.sharding import PartitionSpec as P

MESH = pl.DeviceIdType.MESH
F32 = jnp.float32
BF16 = jnp.bfloat16


def layer_norm(values, scale_gain):
    average = jnp.mean(values, axis=-1, keepdims=True)
    centered = values - average
    variance = jnp.mean(centered * centered, axis=-1, keepdims=True)
    return centered / jnp.sqrt(variance + 1e-05) * scale_gain


def activations(raw_pairs, valid_rows, k_valid, in_gain, weight):
    row_count, width_k, channels = raw_pairs.shape
    normed = layer_norm(raw_pairs.astype(F32), in_gain).astype(BF16)
    projected = jnp.dot(
        normed.reshape(row_count * width_k, channels), weight, preferred_element_type=F32
    )
    projected = projected.reshape(row_count, width_k, -1)
    hidden = projected.shape[-1] // 2
    masking = valid_rows.astype(F32)[:, None] * k_valid.astype(F32)[None, :]
    return (
        jax.nn.sigmoid(projected[..., :hidden]) * projected[..., hidden:] * masking[..., None]
    ).astype(BF16)


def local_collectives(
    z_left, z_right, pair_block, row_valid, col_valid, k_valid,
    in_gain, w_left, w_right, w_gate, w_out, out_gain,
):
    left_act = activations(z_left, row_valid, k_valid, in_gain, w_left)
    right_act = activations(z_right, col_valid, k_valid, in_gain, w_right)
    hidden = left_act.shape[2]
    block_rows, block_cols, channels = pair_block.shape
    triangle = jnp.einsum(
        "ikc,jkc->ijc",
        left_act,
        lax.all_gather(right_act, "row", axis=0, tiled=True),
        preferred_element_type=F32,
    )
    tnorm = layer_norm(triangle, out_gain).astype(BF16)
    swapped = lax.all_to_all(tnorm, "row", split_axis=1, concat_axis=0, tiled=True)
    normed_block = layer_norm(pair_block.astype(F32), in_gain).astype(BF16)
    gate_value = jax.nn.sigmoid(
        jnp.dot(normed_block.reshape(-1, channels), w_gate, preferred_element_type=F32)
    )
    outward = jnp.dot(swapped.reshape(-1, hidden), w_out, preferred_element_type=F32)
    return (gate_value * outward).reshape(block_rows, block_cols, channels).astype(BF16)


def sigmoid(value):
    return 0.5 * jnp.tanh(0.5 * value) + 0.5


def normed_rows(raw, gain, averaging):
    centered = raw.astype(F32) - jnp.dot(raw, averaging, preferred_element_type=F32)
    variance = jnp.dot((centered * centered).astype(BF16), averaging, preferred_element_type=F32)
    return (centered * lax.rsqrt(variance + 1e-05) * gain).astype(BF16)


def kernel(
    n,
    z_left, z_right, pair, row_valid, col_valid, k_valid, in_gain, w_left, w_right, w_gate, w_out, out_gain,
    out,
    gathered, left, gate, band, partial, outgoing, incoming,
    got, up_sem, down_sem, side_sem, twin_sem, back_sem, back_got,
):
    rows, width, channels = z_left.shape
    cols = z_right.shape[0]
    per_block = rows * cols
    nz = n // 4
    me = lax.axis_index("row")
    core = lax.rem(me, 2)
    y = lax.rem(me // 2, 2)
    z = me // 4

    def place(pz, py, pc):
        return (pz * 2 + py) * 2 + pc

    barrier = pltpu.get_barrier_semaphore()

    def greet(step, _):
        peer = lax.rem(me + step, n)
        pl.semaphore_signal(barrier, inc=1, device_id={"row": peer}, device_id_type=MESH)
        return 0

    lax.fori_loop(1, n, greet, 0)

    def carry(src, chunk, sem, target):
        return pltpu.make_async_remote_copy(
            src_ref=gathered.at[src, chunk],
            dst_ref=gathered.at[src, chunk],
            send_sem=sem,
            recv_sem=got.at[src, chunk],
            device_id={"row": target},
            device_id_type=MESH,
        )

    def go_up(pz, chunk):
        return carry(place(pz, y, core), chunk, up_sem.at[pz, chunk], lax.rem(me + 4, n))

    def go_down(pz, chunk):
        return carry(place(pz, y, core), chunk, down_sem.at[pz, chunk], lax.rem(me + n - 4, n))

    def go_side(pz, chunk):
        return carry(place(pz, y, core), chunk, side_sem.at[pz, chunk], place(z, 1 - y, core))

    def go_twin(pz, py, chunk):
        return carry(
            place(pz, py, core), chunk, twin_sem.at[pz * 2 + py, chunk], place(z, y, 1 - core)
        )

    def give_back(src):
        return pltpu.make_async_remote_copy(
            src_ref=outgoing.at[src],
            dst_ref=incoming.at[me],
            send_sem=back_sem.at[src],
            recv_sem=back_got.at[me],
            device_id={"row": src},
            device_id_type=MESH,
        )

    def wait_got(src, chunk):
        carry(src, chunk, up_sem.at[0, 0], place(z, y, 1 - core)).wait_recv()

    averaging = jnp.full((channels, channels), 1.0 / channels, BF16)
    gain = in_gain[...]

    across = lax.broadcasted_iota(jnp.int32, (width, width), 0)
    along = lax.broadcasted_iota(jnp.int32, (width, width), 1)
    spread = jnp.where(across == along, k_valid[...].astype(F32), 0.0).astype(BF16)
    k_mask = jnp.dot(spread, jnp.ones((width, channels), BF16), preferred_element_type=F32)

    for chunk in range(cols):
        projected = jnp.dot(
            normed_rows(z_right[chunk], gain, averaging), w_right[...], preferred_element_type=F32
        )
        valid = col_valid[chunk].astype(F32)
        gathered[me, chunk] = (
            sigmoid(projected[:, :channels]) * projected[:, channels:] * (k_mask * valid)
        ).astype(BF16)
        if chunk == 0:
            pl.semaphore_wait(barrier, n - 1)

        @pl.when(z + 1 < nz)
        def _():
            go_up(z, chunk).start()

        @pl.when(z > 0)
        def _():
            go_down(z, chunk).start()

        go_side(z, chunk).start()
        go_twin(z, y, chunk).start()

    def left_rows(quarter):
        def one(step, _):
            i = quarter * (rows // cols) + step
            projected = jnp.dot(
                normed_rows(z_left[i], gain, averaging), w_left[...], preferred_element_type=F32
            )
            valid = row_valid[i].astype(F32)
            left[i] = (
                (sigmoid(projected[:, :channels]) * projected[:, channels:] * valid)
                .astype(BF16)
                .astype(F32)
            )
            return 0

        lax.fori_loop(0, rows // cols, one, 0)

    def gate_rows(quarter):
        size = pair.shape[0] // cols
        span = pl.ds(pl.multiple_of(quarter * size, size), size)
        normed = normed_rows(pair[span, :], gain, averaging)
        gate[span, :] = sigmoid(jnp.dot(normed, w_gate[...], preferred_element_type=F32))

    pick_row = lax.broadcasted_iota(jnp.int32, (per_block, per_block * 8), 0)
    pick_col = lax.broadcasted_iota(jnp.int32, (per_block, per_block * 8), 1)
    summing = (pick_col // 8 == pick_row).astype(BF16)
    group = 4

    def triangle_block(src):
        band[...] = gathered[src].astype(F32)

        def some_rows(at, _):
            def some_k(kk, totals):
                totals = list(totals)
                for part in range(4):
                    span = pl.ds(pl.multiple_of(kk * 32 + part * 8, 8), 8)
                    rights = [band[j, span, :] for j in range(cols)]
                    for ii in range(group):
                        one_left = left[at * group + ii, span, :]
                        for j in range(cols):
                            totals[ii * cols + j] = totals[ii * cols + j] + one_left * rights[j]
                return tuple(totals)

            totals = lax.fori_loop(
                0, width // 32, some_k,
                tuple(jnp.zeros((8, channels), F32) for _ in range(group * cols)),
            )
            for index, total in enumerate(totals):
                partial[pl.ds(pl.multiple_of((at * group * cols + index) * 8, 8), 8), :] = total
            return 0

        lax.fori_loop(0, rows // group, some_rows, 0)
        whole = partial[...]
        high = whole.astype(BF16)
        low = (whole - high.astype(F32)).astype(BF16)
        triangle = jnp.dot(summing, high, preferred_element_type=F32) + jnp.dot(
            summing, low, preferred_element_type=F32
        )
        centered = triangle - jnp.mean(triangle, axis=-1, keepdims=True)
        variance = jnp.mean(centered * centered, axis=-1, keepdims=True)
        tnorm = (centered * lax.rsqrt(variance + 1e-05) * out_gain[...]).astype(BF16)
        outward = jnp.dot(tnorm, w_out[...], preferred_element_type=F32).astype(BF16)

        @pl.when(src == me)
        def _():
            incoming[me] = outward

        @pl.when(src != me)
        def _():
            outgoing[src] = outward
            give_back(src).start()

    def step(t, _):
        distance = t // cols
        chunk = lax.rem(t, cols)

        def arrivals(way, _):
            sign = 1 - 2 * way
            pz = z + (distance + 1) * sign

            @pl.when((pz >= 0) & (pz < nz))
            def _():
                wait_got(place(pz, y, core), chunk)

                @pl.when((way == 0) & (z > 0))
                def _():
                    go_down(pz, chunk).start()

                @pl.when((way == 1) & (z + 1 < nz))
                def _():
                    go_up(pz, chunk).start()

                go_side(pz, chunk).start()
                go_twin(pz, y, chunk).start()

            qz = z + distance * sign

            @pl.when((qz >= 0) & (qz < nz) & ((distance > 0) | (way == 0)))
            def _():
                wait_got(place(qz, 1 - y, core), chunk)
                go_twin(qz, 1 - y, chunk).start()

            return 0

        lax.fori_loop(0, 2, arrivals, 0)

        @pl.when(distance == 0)
        def _():
            left_rows(chunk)

        @pl.when(distance == 1)
        def _():
            gate_rows(chunk)

        def blocks(way, _):
            before = distance - 1
            pz = z + before * (1 - 2 * way)
            across_y = lax.rem(chunk, 2)
            across_core = chunk // 2

            @pl.when((pz >= 0) & (pz < nz) & ((before > 0) | ((before == 0) & (way == 0))))
            def _():
                py = lax.rem(y + across_y, 2)
                src = place(pz, py, lax.rem(core + across_core, 2))

                @pl.when(across_core == 1)
                def _():
                    for c in range(cols):
                        wait_got(src, c)

                triangle_block(src)

            return 0

        lax.fori_loop(0, 2, blocks, 0)
        return 0

    lax.fori_loop(0, (nz + 1) * cols, step, 0)

    def finish(src, _):
        @pl.when(src != me)
        def _():
            pltpu.make_async_remote_copy(
                src_ref=outgoing.at[src],
                dst_ref=incoming.at[src],
                send_sem=back_sem.at[src],
                recv_sem=back_got.at[src],
                device_id={"row": src},
                device_id_type=MESH,
            ).wait_recv()

        span = pl.ds(pl.multiple_of(src * per_block, per_block), per_block)
        out[span, :] = (gate[span, :] * incoming[src].astype(F32)).astype(BF16)
        return 0

    lax.fori_loop(0, n, finish, 0)

    def settle(pz, _):
        for chunk in range(cols):
            @pl.when((pz <= z) & (z + 1 < nz))
            def _():
                go_up(pz, chunk).wait_send()

            @pl.when((pz >= z) & (z > 0))
            def _():
                go_down(pz, chunk).wait_send()

            go_side(pz, chunk).wait_send()
            go_twin(pz, 0, chunk).wait_send()
            go_twin(pz, 1, chunk).wait_send()
        return 0

    lax.fori_loop(0, nz, settle, 0)

    def settle_back(src, _):
        @pl.when(src != me)
        def _():
            give_back(src).wait_send()

        return 0

    lax.fori_loop(0, n, settle_back, 0)


def local_kernel(
    n,
    z_left, z_right, pair_block, row_valid, col_valid, k_valid,
    in_gain, w_left, w_right, w_gate, w_out, out_gain,
):
    rows, width, channels = z_left.shape
    cols = z_right.shape[0]
    per_block = rows * cols
    vmem = pl.BlockSpec(memory_space=pltpu.VMEM)
    smem = pl.BlockSpec(memory_space=pltpu.SMEM)
    nz = n // 4
    dma = pltpu.SemaphoreType.DMA
    flat = pl.pallas_call(
        functools.partial(kernel, n),
        out_shape=jax.ShapeDtypeStruct((n * per_block, channels), BF16),
        in_specs=[vmem, vmem, vmem, smem, smem] + [vmem] * 7,
        out_specs=vmem,
        scratch_shapes=[
            pltpu.VMEM((n, cols, width, channels), BF16),
            pltpu.VMEM((rows, width, channels), F32),
            pltpu.VMEM((n * per_block, channels), F32),
            pltpu.VMEM((cols, width, channels), F32),
            pltpu.VMEM((per_block * 8, channels), F32),
            pltpu.VMEM((n, per_block, channels), BF16),
            pltpu.VMEM((n, per_block, channels), BF16),
            dma((n, cols)),
            dma((nz, cols)),
            dma((nz, cols)),
            dma((nz, cols)),
            dma((nz * 2, cols)),
            dma((n,)),
            dma((n,)),
        ],
        compiler_params=pltpu.CompilerParams(
            collective_id=0, has_side_effects=True, vmem_limit_bytes=40 * 1024 * 1024
        ),
    )(
        z_left, z_right, pair_block.reshape(-1, channels), row_valid, col_valid,
        k_valid.reshape(1, -1), in_gain.reshape(1, -1), w_left, w_right, w_gate, w_out,
        out_gain.reshape(1, -1),
    )
    return flat.reshape(pair_block.shape)


def fits(n, z_left, z_right):
    rows, width, channels = z_left.shape
    cols = z_right.shape[0]
    return (
        n % 4 == 0
        and cols == 4
        and rows % 4 == 0
        and width % 32 == 0
        and n * cols * width * channels * 2 <= 8 * 1024 * 1024
    )


def solution(mesh):
    n = mesh.shape["row"]

    def local(*arrays):
        if fits(n, arrays[0], arrays[1]):
            return local_kernel(n, *arrays)
        return local_collectives(*arrays)

    placed = (
        P(("parts", "row"), None, None),
        P(("parts", "row"), None, None),
        P("parts", "row", None),
        P(("parts", "row")),
        P(("parts", "row")),
        P("parts"),
        P(),
        P(),
        P(),
        P(),
        P(),
        P(),
    )
    return jax.shard_map(
        local, mesh=mesh, in_specs=placed, out_specs=P("parts", "row", None), check_vma=False
    )
```

time: 100 us -> 55.9 us (0.56)
  waiting for transfers between devices: 55.7 us -> 0 us
  Pallas kernels: 0 us -> 47.7 us
  between operations: 13.6 us -> 0.04 us
  other arithmetic: 9.51 us -> 0 us
  matrix products: 7.54 us -> 0 us
  starting transfers between devices: 3.71 us -> 0 us
  local copies, waits for them, and re-layouts: 9.19 us -> 7.73 us
    pallas_call x0 -> x1, Pallas kernels: none -> 47.7 us  [local_kernel(): pl.pallas_call(functools.partial(kernel, n), out_shape=jax.ShapeDtypeStru...]
    all_gather x1 -> x0, waiting for transfers between devices: 47.2 us -> none  [local(): lax.all_gather(right_act, 'row', axis=0, tiled=True)]
    all_to_all x1 -> x0, waiting for transfers between devices: 8.54 us -> none  [local(): lax.all_to_all(tnorm, 'row', split_axis=1, concat_axis=0, tiled=True)]
    unnamed x16 -> x25, local copies, waits for them, and re-layouts: 0.07 us -> 7.73 us
    dot_general x5 -> x0, matrix products: 7.54 us -> none  [the longest x1 3.4 us: local(): jnp.einsum('ikc,jkc->ijc', left_act, lax.all_gather(right_act, 'row', axi...]
    all_gather x1 -> x0, local copies, waits for them, and re-layouts: 6.82 us -> none  [local(): lax.all_gather(right_act, 'row', axis=0, tiled=True)]
    reduce_sum x7 -> x0, other arithmetic: 5.34 us -> none  [the longest x4 3.55 us: layer_norm(): variance = jnp.mean(centered * centered, axis=-1, keepdims=True)]
    convert_element_type x7 -> x0, other arithmetic: 3.93 us -> none  [the longest x2 1.63 us: activations(): return (jax.nn.sigmoid(projected[..., :hidden]) * projected[..., hidden:]...]
  transfers between devices with their start and end apart: 2 -> 0, of which waited for: 2 -> 0; matrix products, arithmetic and copies ran while one was open for 7% -> 0% of each run, Pallas kernels for 0% -> 0%
where the time goes in v1:
time: 55.9 us; the launch traced here: 55.4 us
  Pallas kernels  47.7 us (85%)
  local copies, waits for them, and re-layouts  7.73 us (14%)
    pallas_call x1, Pallas kernels, local_kernel(): pl.pallas_call(functools.partial(kernel, n), out_shape=jax.ShapeDtypeStru...  47.7 us
    unnamed x25, local copies, waits for them, and re-layouts  7.73 us

profile of v1, /device:TPU:1, one launch (start us, length us, event | category | flops | bytes accessed | tf_op | source)
XLA Modules:
  0.0 55.4 jit_solution(7018612558325597347)
XLA Ops:
  0.0 0.0 copy-start.9
  0.0 0.0 copy-start.10
  0.0 0.0 copy-start.11
  0.0 0.0 copy-start.7
  0.0 0.0 copy-start.8
  0.0 0.6 %copy-done.9 = s32[4]{0:T(128)S(1)} copy-done((s32[4]{0:T(128)S(1)}, s32[4]{0:T(128)}, u32[]{:S(2)}) %copy-start.9) | copy-done | bytes 40
  0.7 0.0 copy-done.10
  0.7 0.0 copy-done.11
  0.7 0.0 copy-done.7
  0.7 0.0 copy-done.8
  0.7 0.0 copy-start
  0.7 1.2 %copy-done = bf16[16,256,128]{2,1,0:T(8,128)(2,1)S(1)} copy-done((bf16[16,256,128]{2,1,0:T(8,128)(2,1)S(1)}, bf16[16,256,128]{2,1,0:T(8,128)(2,1)}, u32[]{:S(2)}) %copy-start) | copy-done | bytes 1048600
  2.0 0.0 copy-start.1
  2.0 0.9 %copy-done.1 = bf16[4,256,128]{2,1,0:T(8,128)(2,1)S(1)} copy-done((bf16[4,256,128]{2,1,0:T(8,128)(2,1)S(1)}, bf16[4,256,128]{2,1,0:T(8,128)(2,1)}, u32[]{:S(2)}) %copy-start.1) | copy-done | bytes 262168
  2.9 0.0 copy-start.2
  2.9 0.9 %copy-done.2 = bf16[256,4,128]{2,1,0:T(4,128)(2,1)S(1)} copy-done((bf16[256,4,128]{2,1,0:T(4,128)(2,1)S(1)}, bf16[256,4,128]{2,1,0:T(4,128)(2,1)}, u32[]{:S(2)}) %copy-start.2) | copy-done | bytes 262168
  3.9 0.0 copy-start.3
  3.9 0.8 %copy-done.3 = bf16[128,256]{1,0:T(8,128)(2,1)S(1)} copy-done((bf16[128,256]{1,0:T(8,128)(2,1)S(1)}, bf16[128,256]{1,0:T(8,128)(2,1)}, u32[]{:S(2)}) %copy-start.3) | copy-done | bytes 65560
  4.7 0.0 copy-start.4
  4.7 0.8 %copy-done.4 = bf16[128,256]{1,0:T(8,128)(2,1)S(1)} copy-done((bf16[128,256]{1,0:T(8,128)(2,1)S(1)}, bf16[128,256]{1,0:T(8,128)(2,1)}, u32[]{:S(2)}) %copy-start.4) | copy-done | bytes 65560
  5.5 0.0 copy-start.5
  5.5 0.8 %copy-done.5 = bf16[128,128]{1,0:T(8,128)(2,1)S(1)} copy-done((bf16[128,128]{1,0:T(8,128)(2,1)S(1)}, bf16[128,128]{1,0:T(8,128)(2,1)}, u32[]{:S(2)}) %copy-start.5) | copy-done | bytes 32792
  6.3 0.0 copy-start.6
  6.3 0.8 %copy-done.6 = bf16[128,128]{1,0:T(8,128)(2,1)S(1)} copy-done((bf16[128,128]{1,0:T(8,128)(2,1)S(1)}, bf16[128,128]{1,0:T(8,128)(2,1)}, u32[]{:S(2)}) %copy-start.6) | copy-done | bytes 32792
  7.1 47.7 %shard_map.118 = bf16[1024,128]{1,0:T(8,128)(2,1)S(1)} custom-call(bf16[16,256,128]{2,1,0:T(8,128)(2,1)S(1)} %copy-done, bf16[4,256,128]{2,1,0:T(8,128)(2,1)S(1)} %copy-done.1, bf16[1024,128]{1,0:T(8,128)(2,1)S(1)} %bitcast.6, s32[16]{0:T(128)S(1)} %copy-done.8, s32[4]{0:T(128)S(1)} %copy-done.9, s32[1,256]{1,0:T(1,128)S(1)} %bitcast.7, ...), custom_call_target="tpu_custom_call" | custom-call | tf_op jit(solution)/shard_map/pallas_call | solution.py:360
  54.7 0.7 %copy.14 = bf16[256,4,128]{2,1,0:T(4,128)(2,1)} copy(bf16[256,4,128]{2,1,0:T(4,128)(2,1)S(1)} %bitcast.5) | data formatting | bytes 524288
Async XLA Ops:
  0.0 0.7 %copy-start.9 = (s32[4]{0:T(128)S(1)}, s32[4]{0:T(128)}, u32[]{:S(2)}) copy-start(s32[4]{0:T(128)} %col_valid.1) | copy-start | bytes 52
  0.0 0.7 %copy-start.10 = (f32[128]{0:T(128)S(1)}, f32[128]{0:T(128)}, u32[]{:S(2)}) copy-start(f32[128]{0:T(128)} %param.18) | copy-start | bytes 1540
  0.0 0.7 %copy-start.11 = (f32[128]{0:T(128)S(1)}, f32[128]{0:T(128)}, u32[]{:S(2)}) copy-start(f32[128]{0:T(128)} %param.23) | copy-start | bytes 1540
  0.0 0.7 %copy-start.7 = (s32[256]{0:T(256)S(1)}, s32[256]{0:T(256)}, u32[]{:S(2)}) copy-start(s32[256]{0:T(256)} %param.17) | copy-start | bytes 3076
  0.0 0.7 %copy-start.8 = (s32[16]{0:T(128)S(1)}, s32[16]{0:T(128)}, u32[]{:S(2)}) copy-start(s32[16]{0:T(128)} %row_valid.1) | copy-start | bytes 196
  0.7 1.2 %copy-start = (bf16[16,256,128]{2,1,0:T(8,128)(2,1)S(1)}, bf16[16,256,128]{2,1,0:T(8,128)(2,1)}, u32[]{:S(2)}) copy-start(bf16[16,256,128]{2,1,0:T(8,128)(2,1)} %z_left.1) | copy-start | bytes 3145732
  2.0 0.9 %copy-start.1 = (bf16[4,256,128]{2,1,0:T(8,128)(2,1)S(1)}, bf16[4,256,128]{2,1,0:T(8,128)(2,1)}, u32[]{:S(2)}) copy-start(bf16[4,256,128]{2,1,0:T(8,128)(2,1)} %z_right.1) | copy-start | bytes 786436
  2.9 0.9 %copy-start.2 = (bf16[256,4,128]{2,1,0:T(4,128)(2,1)S(1)}, bf16[256,4,128]{2,1,0:T(4,128)(2,1)}, u32[]{:S(2)}) copy-start(bf16[256,4,128]{2,1,0:T(4,128)(2,1)} %param.14) | copy-start | bytes 786436
  3.9 0.8 %copy-start.3 = (bf16[128,256]{1,0:T(8,128)(2,1)S(1)}, bf16[128,256]{1,0:T(8,128)(2,1)}, u32[]{:S(2)}) copy-start(bf16[128,256]{1,0:T(8,128)(2,1)} %w_left.1) | copy-start | bytes 196612
  4.7 0.8 %copy-start.4 = (bf16[128,256]{1,0:T(8,128)(2,1)S(1)}, bf16[128,256]{1,0:T(8,128)(2,1)}, u32[]{:S(2)}) copy-start(bf16[128,256]{1,0:T(8,128)(2,1)} %w_right.1) | copy-start | bytes 196612
  5.5 0.8 %copy-start.5 = (bf16[128,128]{1,0:T(8,128)(2,1)S(1)}, bf16[128,128]{1,0:T(8,128)(2,1)}, u32[]{:S(2)}) copy-start(bf16[128,128]{1,0:T(8,128)(2,1)} %w_gate.1) | copy-start | bytes 98308
  6.3 0.8 %copy-start.6 = (bf16[128,128]{1,0:T(8,128)(2,1)S(1)}, bf16[128,128]{1,0:T(8,128)(2,1)}, u32[]{:S(2)}) copy-start(bf16[128,128]{1,0:T(8,128)(2,1)} %w_out.1) | copy-start | bytes 98308

commit v2 on v1

--- a/solution.py
+++ b/solution.py
@@ -69,10 +69,13 @@
 
 def kernel(
     n,
-    z_left, z_right, pair, row_valid, col_valid, k_valid, in_gain, w_left, w_right, w_gate, w_out, out_gain,
+    z_left_hbm, z_right_hbm, pair_hbm, row_valid_hbm, col_valid_hbm, k_valid_hbm,
+    in_gain_hbm, w_left_hbm, w_right_hbm, w_gate_hbm, w_out_hbm, out_gain_hbm,
     out,
-    gathered, left, gate, band, partial, outgoing, incoming,
-    got, up_sem, down_sem, side_sem, twin_sem, back_sem, back_got,
+    z_left, z_right, pair, row_valid, col_valid, k_valid,
+    in_gain, w_left, w_right, w_gate, w_out, out_gain,
+    gathered, left, gate, partial, summing, outgoing, incoming,
+    got, up_sem, down_sem, side_sem, twin_sem, back_sem, back_got, load_sem,
 ):
     rows, width, channels = z_left.shape
     cols = z_right.shape[0]
@@ -86,6 +89,24 @@
     def place(pz, py, pc):
         return (pz * 2 + py) * 2 + pc
 
+    loads = {}
+    for index, (name, source, target) in enumerate((
+        ("z_right", z_right_hbm, z_right),
+        ("w_right", w_right_hbm, w_right),
+        ("in_gain", in_gain_hbm, in_gain),
+        ("k_valid", k_valid_hbm, k_valid),
+        ("col_valid", col_valid_hbm, col_valid),
+        ("z_left", z_left_hbm, z_left),
+        ("w_left", w_left_hbm, w_left),
+        ("row_valid", row_valid_hbm, row_valid),
+        ("pair", pair_hbm, pair),
+        ("w_gate", w_gate_hbm, w_gate),
+        ("w_out", w_out_hbm, w_out),
+        ("out_gain", out_gain_hbm, out_gain),
+    )):
+        loads[name] = pltpu.make_async_copy(source, target, load_sem.at[index])
+        loads[name].start()
+
     barrier = pltpu.get_barrier_semaphore()
 
     def greet(step, _):
@@ -132,6 +153,8 @@
     def wait_got(src, chunk):
         carry(src, chunk, up_sem.at[0, 0], place(z, y, 1 - core)).wait_recv()
 
+    for name in ("z_right", "w_right", "in_gain", "k_valid", "col_valid"):
+        loads[name].wait()
     averaging = jnp.full((channels, channels), 1.0 / channels, BF16)
     gain = in_gain[...]
 
@@ -162,6 +185,9 @@
         go_side(z, chunk).start()
         go_twin(z, y, chunk).start()
 
+    for name in ("z_left", "w_left", "row_valid", "pair", "w_gate", "w_out", "out_gain"):
+        loads[name].wait()
+
     def left_rows(quarter):
         def one(step, _):
             i = quarter * (rows // cols) + step
@@ -170,10 +196,8 @@
             )
             valid = row_valid[i].astype(F32)
             left[i] = (
-                (sigmoid(projected[:, :channels]) * projected[:, channels:] * valid)
-                .astype(BF16)
-                .astype(F32)
-            )
+                sigmoid(projected[:, :channels]) * projected[:, channels:] * valid
+            ).astype(BF16)
             return 0
 
         lax.fori_loop(0, rows // cols, one, 0)
@@ -184,41 +208,36 @@
         normed = normed_rows(pair[span, :], gain, averaging)
         gate[span, :] = sigmoid(jnp.dot(normed, w_gate[...], preferred_element_type=F32))
 
-    pick_row = lax.broadcasted_iota(jnp.int32, (per_block, per_block * 8), 0)
-    pick_col = lax.broadcasted_iota(jnp.int32, (per_block, per_block * 8), 1)
-    summing = (pick_col // 8 == pick_row).astype(BF16)
-    group = 4
+    depth = 32
+    pick_row = lax.broadcasted_iota(jnp.int32, (per_block, per_block * depth), 0)
+    pick_col = lax.broadcasted_iota(jnp.int32, (per_block, per_block * depth), 1)
+    summing[...] = (pick_col // depth == pick_row).astype(BF16)
+    group = 2
 
     def triangle_block(src):
-        band[...] = gathered[src].astype(F32)
-
         def some_rows(at, _):
-            def some_k(kk, totals):
-                totals = list(totals)
-                for part in range(4):
-                    span = pl.ds(pl.multiple_of(kk * 32 + part * 8, 8), 8)
-                    rights = [band[j, span, :] for j in range(cols)]
-                    for ii in range(group):
-                        one_left = left[at * group + ii, span, :]
-                        for j in range(cols):
-                            totals[ii * cols + j] = totals[ii * cols + j] + one_left * rights[j]
-                return tuple(totals)
-
-            totals = lax.fori_loop(
-                0, width // 32, some_k,
-                tuple(jnp.zeros((8, channels), F32) for _ in range(group * cols)),
-            )
-            for index, total in enumerate(totals):
-                partial[pl.ds(pl.multiple_of((at * group * cols + index) * 8, 8), 8), :] = total
+            totals = [[] for _ in range(group * cols)]
+            for part in range(width // depth):
+                span = pl.ds(part * depth, depth)
+                rights = [gathered[src, j, span, :] for j in range(cols)]
+                for ii in range(group):
+                    one_left = left[at * group + ii, span, :]
+                    for j in range(cols):
+                        pile = totals[ii * cols + j]
+                        term, level = one_left * rights[j], 0
+                        while pile and pile[-1][1] == level:
+                            term, level = pile.pop()[0] + term, level + 1
+                        pile.append((term, level))
+            for index, pile in enumerate(totals):
+                total = pile.pop()[0]
+                while pile:
+                    total = pile.pop()[0] + total
+                first = pl.multiple_of((at * group * cols + index) * depth, depth)
+                partial[pl.ds(first, depth), :] = total
             return 0
 
         lax.fori_loop(0, rows // group, some_rows, 0)
-        whole = partial[...]
-        high = whole.astype(BF16)
-        low = (whole - high.astype(F32)).astype(BF16)
-        triangle = jnp.dot(summing, high, preferred_element_type=F32) + jnp.dot(
-            summing, low, preferred_element_type=F32
-        )
+        triangle = jnp.dot(summing[...], partial[...], preferred_element_type=F32)
         centered = triangle - jnp.mean(triangle, axis=-1, keepdims=True)
         variance = jnp.mean(centered * centered, axis=-1, keepdims=True)
         tnorm = (centered * lax.rsqrt(variance + 1e-05) * out_gain[...]).astype(BF16)
@@ -353,21 +372,31 @@
     rows, width, channels = z_left.shape
     cols = z_right.shape[0]
     per_block = rows * cols
-    vmem = pl.BlockSpec(memory_space=pltpu.VMEM)
-    smem = pl.BlockSpec(memory_space=pltpu.SMEM)
     nz = n // 4
     dma = pltpu.SemaphoreType.DMA
     flat = pl.pallas_call(
         functools.partial(kernel, n),
         out_shape=jax.ShapeDtypeStruct((n * per_block, channels), BF16),
-        in_specs=[vmem, vmem, vmem, smem, smem] + [vmem] * 7,
-        out_specs=vmem,
+        in_specs=[pl.BlockSpec(memory_space=pl.ANY)] * 12,
+        out_specs=pl.BlockSpec(memory_space=pltpu.VMEM),
         scratch_shapes=[
+            pltpu.VMEM(z_left.shape, BF16),
+            pltpu.VMEM(z_right.shape, BF16),
+            pltpu.VMEM((n * per_block, channels), BF16),
+            pltpu.SMEM(row_valid.shape, jnp.int32),
+            pltpu.SMEM(col_valid.shape, jnp.int32),
+            pltpu.VMEM((1, width), jnp.int32),
+            pltpu.VMEM((1, channels), F32),
+            pltpu.VMEM(w_left.shape, BF16),
+            pltpu.VMEM(w_right.shape, BF16),
+            pltpu.VMEM(w_gate.shape, BF16),
+            pltpu.VMEM(w_out.shape, BF16),
+            pltpu.VMEM((1, channels), F32),
             pltpu.VMEM((n, cols, width, channels), BF16),
-            pltpu.VMEM((rows, width, channels), F32),
+            pltpu.VMEM((rows, width, channels), BF16),
             pltpu.VMEM((n * per_block, channels), F32),
-            pltpu.VMEM((cols, width, channels), F32),
-            pltpu.VMEM((per_block * 8, channels), F32),
+            pltpu.VMEM((per_block * 32, channels), BF16),
+            pltpu.VMEM((per_block, per_block * 32), BF16),
             pltpu.VMEM((n, per_block, channels), BF16),
             pltpu.VMEM((n, per_block, channels), BF16),
             dma((n, cols)),
@@ -377,9 +406,10 @@
             dma((nz * 2, cols)),
             dma((n,)),
             dma((n,)),
+            dma((12,)),
         ],
         compiler_params=pltpu.CompilerParams(
-            collective_id=0, has_side_effects=True, vmem_limit_bytes=40 * 1024 * 1024
+            collective_id=0, has_side_effects=True, vmem_limit_bytes=60 * 1024 * 1024
         ),
     )(
         z_left, z_right, pair_block.reshape(-1, channels), row_valid, col_valid,

time: 55.9 us -> 48.1 us (0.86)
  local copies, waits for them, and re-layouts: 7.73 us -> 1.74 us
  Pallas kernels: 47.7 us -> 46.2 us
    unnamed x25 -> x1, local copies, waits for them, and re-layouts: 7.73 us -> 1.74 us
    pallas_call x1, Pallas kernels: 47.7 us -> 46.2 us  [local_kernel(): pl.pallas_call(functools.partial(kernel, n), out_shape=jax.ShapeDtypeStru...]
where the time goes in v2:
time: 48.1 us; the launch traced here: 48 us
  Pallas kernels  46.2 us (96%)
  local copies, waits for them, and re-layouts  1.74 us (4%)
    pallas_call x1, Pallas kernels, local_kernel(): pl.pallas_call(functools.partial(kernel, n), out_shape=jax.ShapeDtypeStru...  46.2 us
    unnamed x1, local copies, waits for them, and re-layouts  1.74 us

profile of v2, /device:TPU:1, one launch (start us, length us, event | category | flops | bytes accessed | tf_op | source)
XLA Modules:
  0.0 48.0 jit_solution(3776616291818783433)
XLA Ops:
  0.0 46.2 %shard_map.118 = bf16[1024,128]{1,0:T(8,128)(2,1)} custom-call(bf16[16,256,128]{2,1,0:T(8,128)(2,1)} %z_left_hbm.1, bf16[4,256,128]{2,1,0:T(8,128)(2,1)} %z_right_hbm.1, bf16[1024,128]{1,0:T(8,128)(2,1)} %bitcast.6, s32[16]{0:T(128)} %row_valid_hbm.1, s32[4]{0:T(128)} %col_valid_hbm.1, s32[1,256]{1,0:T(1,128)} %bitcast.7, f32[1,128]{1,0:T(1,128)} %bitcast.8, ...), custom_call_target="tpu_custom_call" | custom-call | tf_op jit(solution)/shard_map/pallas_call | solution.py:377
  46.2 1.7 %copy.14 = bf16[256,4,128]{2,1,0:T(4,128)(2,1)} copy(bf16[256,4,128]{2,1,0:T(4,128)(2,1)} %bitcast.5) | data formatting | bytes 524288

commit v3 on v2

--- a/solution.py
+++ b/solution.py
@@ -214,43 +214,52 @@
     summing[...] = (pick_col // depth == pick_row).astype(BF16)
     group = 2
 
-    def triangle_block(src):
+    def triangle_pair(first, second):
+        pair_of = (first, second)
+
         def some_rows(at, _):
-            totals = [[] for _ in range(group * cols)]
-            for part in range(width // depth):
-                span = pl.ds(part * depth, depth)
-                rights = [gathered[src, j, span, :] for j in range(cols)]
-                for ii in range(group):
-                    one_left = left[at * group + ii, span, :]
+            totals = [None] * (group * 2 * cols)
+            for part in range(0, width // depth, 2):
+                spans = [pl.ds((part + half) * depth, depth) for half in range(2)]
+                lefts = [[left[at * group + ii, span, :] for span in spans] for ii in range(group)]
+                for which, src in enumerate(pair_of):
                     for j in range(cols):
-                        pile = totals[ii * cols + j]
-                        term, level = one_left * rights[j], 0
-                        while pile and pile[-1][1] == level:
-                            term, level = pile.pop()[0] + term, level + 1
-                        pile.append((term, level))
-            for index, pile in enumerate(totals):
-                total = pile.pop()[0]
-                while pile:
-                    total = pile.pop()[0] + total
-                first = pl.multiple_of((at * group * cols + index) * depth, depth)
-                partial[pl.ds(first, depth), :] = total
+                        rights = [gathered[src, j, span, :] for span in spans]
+                        for ii in range(group):
+                            index = (which * group + ii) * cols + j
+                            term = lefts[ii][0] * rights[0] + lefts[ii][1] * rights[1]
+                            held = totals[index]
+                            totals[index] = term if held is None else held + term
+            for which in range(2):
+                for index in range(group * cols):
+                    place_at = pl.multiple_of((at * group * cols + index) * depth, depth)
+                    partial[which, pl.ds(place_at, depth), :] = totals[which * group * cols + index]
             return 0
 
         lax.fori_loop(0, rows // group, some_rows, 0)
-        triangle = jnp.dot(summing[...], partial[...], preferred_element_type=F32)
+        triangle = jnp.concatenate(
+            [
+                jnp.dot(summing[...], partial[which], preferred_element_type=F32)
+                for which in range(2)
+            ],
+            axis=0,
+        )
         centered = triangle - jnp.mean(triangle, axis=-1, keepdims=True)
         variance = jnp.mean(centered * centered, axis=-1, keepdims=True)
         tnorm = (centered * lax.rsqrt(variance + 1e-05) * out_gain[...]).astype(BF16)
         outward = jnp.dot(tnorm, w_out[...], preferred_element_type=F32).astype(BF16)
 
-        @pl.when(src == me)
-        def _():
-            incoming[me] = outward
-
-        @pl.when(src != me)
-        def _():
-            outgoing[src] = outward
-            give_back(src).start()
+        @pl.when(first == me)
+        def _():
+            incoming[me] = outward[:per_block]
+
+        @pl.when(first != me)
+        def _():
+            outgoing[first] = outward[:per_block]
+            give_back(first).start()
+
+        outgoing[second] = outward[per_block:]
+        give_back(second).start()
 
     def step(t, _):
         distance = t // cols
@@ -294,30 +303,24 @@
         def _():
             gate_rows(chunk)
 
-        def blocks(way, _):
-            before = distance - 1
-            pz = z + before * (1 - 2 * way)
-            across_y = lax.rem(chunk, 2)
-            across_core = chunk // 2
-
-            @pl.when((pz >= 0) & (pz < nz) & ((before > 0) | ((before == 0) & (way == 0))))
-            def _():
-                py = lax.rem(y + across_y, 2)
-                src = place(pz, py, lax.rem(core + across_core, 2))
-
-                @pl.when(across_core == 1)
-                def _():
-                    for c in range(cols):
-                        wait_got(src, c)
-
-                triangle_block(src)
-
-            return 0
-
-        lax.fori_loop(0, 2, blocks, 0)
+        late = (chunk < 2).astype(jnp.int32)
+        far = distance - late
+        way = lax.rem(chunk, 2)
+        own = ((far == 0) & (way == 1)).astype(jnp.int32)
+        pz = z + far * (1 - 2 * way)
+        py = lax.rem(y + late * (1 - own), 2)
+
+        @pl.when((distance > 0) & (pz >= 0) & (pz < nz))
+        def _():
+            first = place(pz, py, core)
+            second = place(pz, py, 1 - core)
+            for c in range(cols):
+                wait_got(second, c)
+            triangle_pair(first, second)
+
         return 0
 
-    lax.fori_loop(0, (nz + 1) * cols, step, 0)
+    lax.fori_loop(0, nz * cols + 2, step, 0)
 
     def finish(src, _):
         @pl.when(src != me)
@@ -395,7 +398,7 @@
             pltpu.VMEM((n, cols, width, channels), BF16),
             pltpu.VMEM((rows, width, channels), BF16),
             pltpu.VMEM((n * per_block, channels), F32),
-            pltpu.VMEM((per_block * 32, channels), BF16),
+            pltpu.VMEM((2, per_block * 32, channels), BF16),
             pltpu.VMEM((per_block, per_block * 32), BF16),
             pltpu.VMEM((n, per_block, channels), BF16),
             pltpu.VMEM((n, per_block, channels), BF16),

time: 48.1 us -> 44.6 us (0.927)
  Pallas kernels: 46.2 us -> 42.3 us
    pallas_call x1, Pallas kernels: 46.2 us -> 42.3 us  [local_kernel(): pl.pallas_call(functools.partial(kernel, n), out_shape=jax.ShapeDtypeStru...]
where the time goes in v3:
time: 44.6 us; the launch traced here: 44.1 us
  Pallas kernels  42.3 us (95%)
  local copies, waits for them, and re-layouts  1.74 us (4%)
    pallas_call x1, Pallas kernels, local_kernel(): pl.pallas_call(functools.partial(kernel, n), out_shape=jax.ShapeDtypeStru...  42.3 us
    unnamed x1, local copies, waits for them, and re-layouts  1.74 us

profile of v3, /device:TPU:1, one launch (start us, length us, event | category | flops | bytes accessed | tf_op | source)
XLA Modules:
  0.0 44.1 jit_solution(2692540605720477310)
XLA Ops:
  0.0 42.3 %shard_map.118 = bf16[1024,128]{1,0:T(8,128)(2,1)} custom-call(bf16[16,256,128]{2,1,0:T(8,128)(2,1)} %z_left_hbm.1, bf16[4,256,128]{2,1,0:T(8,128)(2,1)} %z_right_hbm.1, bf16[1024,128]{1,0:T(8,128)(2,1)} %bitcast.6, s32[16]{0:T(128)} %row_valid_hbm.1, s32[4]{0:T(128)} %col_valid_hbm.1, s32[1,256]{1,0:T(1,128)} %bitcast.7, f32[1,128]{1,0:T(1,128)} %bitcast.8, ...), custom_call_target="tpu_custom_call" | custom-call | tf_op jit(solution)/shard_map/pallas_call | solution.py:380
  42.3 1.7 %copy.14 = bf16[256,4,128]{2,1,0:T(4,128)(2,1)} copy(bf16[256,4,128]{2,1,0:T(4,128)(2,1)} %bitcast.5) | data formatting | bytes 524288
